TPU v7x, 512 devices: a whole 4x4x16 slice. The times are simulated.
512 devices in a mesh: sub: 8 (over y, core), front: 64 (over x, z).
Axes of the slice: x: 4, y: 4, z: 16, core: 2. Of those that a mesh axis runs over, the one named last changes fastest.
Arguments:
- rhs_root: float32 [22528, 128], P(('sub', 'front')), may hold values from -6 to 6
- rhs_level: float32 [11264, 128], P(('sub', 'front')), may hold values from -6 to 6
- root_inverse: bfloat16 [22528, 22528], P('front', 'sub'), as said below
- level_inverse: bfloat16 [11264, 11264], P('front', 'sub'), as said below
- coupling_t: bfloat16 [11264, 11264], P('front', 'sub'), may hold values from -0.078125 to 0.078125
- coupling_rows: int32 [64, 88], P('front', 'sub'), may hold values from 0 to 175, as said below
Outputs:
- root_potential: float32 [22528, 128], P(('sub', 'front'))
- level_potential: float32 [11264, 128], P(('sub', 'front'))
Inputs may be any that keep to these rules, and one draw needn't show every extreme that they name: `root_inverse`: zero above the diagonal; diagonal entries between 0.5 and 1.5. `level_inverse`: zero above the diagonal; diagonal entries between 0.5 and 1.5. `coupling_rows`: entry [p, j] lies in the range of 22 blocks that starts at block (j // 11) * 22; the 11 entries of one panel in one range are distinct; every row block is named by some panel.
All inputs are finite; a program needn't handle non-finite values.
Results may differ from a plain program's by a relative error of at most 0.02.
Values may be sent and summed in bfloat16 or wider, within the bound.
A program may use at most 64 MiB of HBM per device.

v0:
```python
import jax
import jax.numpy as jnp
from jax import lax
from jax.sharding import PartitionSpec as P

RB = 128


HIGHEST_PRECISION = lax.Precision.HIGHEST


def gather_columns(pieces):
    return lax.all_gather(pieces, "front", axis=0, tiled=True)


def gather_rows(pieces):
    return lax.all_gather(pieces, "sub", axis=0, tiled=True)


def share_sub(summand):
    return lax.psum_scatter(
        summand.astype(jnp.bfloat16), "sub", scatter_dimension=0, tiled=True
    ).astype(jnp.float32)


def share_front(summand):
    return lax.psum_scatter(summand, "front", scatter_dimension=0, tiled=True)


def transposed_product(matrix, vector):
    return lax.dot_general(
        matrix, vector, (((0,), (0,)), ((), ())), preferred_element_type=jnp.float32
    )


def body(rhs_root, rhs_level, root_inverse, level_inverse, coupling_t, coupling_rows):
    rhs_count = rhs_root.shape[1]
    block_count = root_inverse.shape[1] // RB
    slot_count = coupling_t.shape[1] // RB
    level_cols = gather_columns(rhs_level.astype(jnp.bfloat16))
    forward_level = share_sub(
        jnp.dot(level_inverse, level_cols, preferred_element_type=jnp.float32)
    )
    level_rows = gather_rows(forward_level.astype(jnp.bfloat16))
    local_block = coupling_rows[0] % block_count
    selector = (
        lax.broadcasted_iota(jnp.int32, (block_count, slot_count), 0) == local_block[None, :]
    ).astype(jnp.float32)
    pushed = transposed_product(coupling_t, level_rows).reshape(slot_count, RB, rhs_count)
    update = jnp.einsum("bk,kin->bin", selector, pushed, precision=HIGHEST_PRECISION).reshape(
        block_count * RB, rhs_count
    )
    shifted = rhs_root - share_front(update)
    root_cols = gather_columns(shifted.astype(jnp.bfloat16))
    forward_root = share_sub(jnp.dot(root_inverse, root_cols, preferred_element_type=jnp.float32))
    root_rows = gather_rows(forward_root.astype(jnp.bfloat16))
    root_potential = share_front(transposed_product(root_inverse, root_rows))
    potential_cols = gather_columns(root_potential.astype(jnp.bfloat16))
    picked = potential_cols.reshape(block_count, RB, rhs_count)[local_block]
    pulled = jnp.dot(
        coupling_t, picked.reshape(slot_count * RB, rhs_count), preferred_element_type=jnp.float32
    )
    corrected = forward_level - share_sub(pulled)
    corrected_rows = gather_rows(corrected.astype(jnp.bfloat16))
    level_potential = share_front(transposed_product(level_inverse, corrected_rows))
    return (root_potential, level_potential)


def solution(mesh):
    return jax.shard_map(
        body,
        mesh=mesh,
        in_specs=(
            P(("sub", "front"), None),
            P(("sub", "front"), None),
            P("front", "sub"),
            P("front", "sub"),
            P("front", "sub"),
            P("front", "sub"),
        ),
        out_specs=(P(("sub", "front"), None), P(("sub", "front"), None)),
        check_vma=False,
    )
```

profile of v0, /device:TPU:1, one launch (start us, length us, event | category | flops | bytes accessed | tf_op | source)
XLA Modules:
  0.0 1134.1 jit_solution(15586352353190416821)
XLA Ops:
  7.2 0.0 copy-start
  7.2 0.0 copy-start.1
  7.2 0.0 all-reduce.13.cloned.1.call-start
  7.2 0.8 convert_bitcast_fusion.1
  8.0 77.6 %all-gather = bf16[64,22,128]{2,1,0:T(8,128)(2,1)S(1)} all-gather(bf16[1,22,128]{2,1,0:T(8,128)(2,1)S(1)} %convert_bitcast_fusion.1), channel_id=1, replica_groups=mesh['sub'=8,'front'=64] {'front'}, dimensions={0}, use_global_device_ids=true | all-gather | bytes 366080 | tf_op jit(solution)/shard_map/all_gather | solution.py:13
  85.6 0.1 reshape.65
  85.8 1.3 convolution_convert_fusion.2
  87.1 37.4 %fusion = bf16[32,128]{1,0:T(8,128)(2,1)S(1)} fusion(bf16[176,128]{1,0:T(8,128)(2,1)S(1)} %convolution_convert_fusion.2), kind=kCustom, calls=%all-reduce-scatter | all-reduce-scatter fusion | flops 32769 | bytes 55296
  124.5 3.5 collective-permute-start
  128.0 1.4 collective-permute-start.1
  129.4 5.2 collective-permute-start.2
  134.7 1.3 dynamic-slice.14
  136.6 0.0 collective-permute-done
  136.6 0.0 collective-permute-done.1
  136.7 0.4 concatenate
  137.1 12.8 %all-gather.1 = bf16[8,22,128]{2,1,0:T(8,128)(2,1)S(1)} all-gather(bf16[1,22,128]{2,1,0:T(8,128)(2,1)S(1)} %fusion.14), channel_id=1, replica_groups=mesh['sub'=8,'front'=64] {'sub'}, dimensions={0}, use_global_device_ids=true | all-gather | bytes 50688 | tf_op jit(solution)/shard_map/all_gather | solution.py:17
  150.0 0.3 convolution_bitcast_fusion.2
  150.3 0.3 copy.17
  150.6 1.2 fusion.6
  151.8 0.0 copy-start.5
  151.8 0.3 copy.19
  152.1 0.0 copy-start.4
  152.1 122.0 %fusion.1 = f32[48,128]{1,0:T(8,128)S(1)} fusion(f32[2816,128]{1,0:T(8,128)S(1)} %bitcast.60), kind=kCustom, calls=%all-reduce-scatter.1 | all-reduce-scatter fusion | flops 393217 | bytes 1468416
  274.1 1.3 collective-permute-start.8
  275.4 1.9 collective-permute-start.3
  277.3 1.3 collective-permute-start.4
  278.6 1.3 collective-permute-start.5
  279.9 1.3 collective-permute-start.6
  281.2 1.3 collective-permute-start.7
  282.5 0.6 fusion.17
  283.8 0.0 collective-permute-done.4
  283.8 0.9 concatenate.1
  284.8 92.4 %all-gather.2 = bf16[64,44,128]{2,1,0:T(8,128)(2,1)S(1)} all-gather(bf16[1,44,128]{2,1,0:T(8,128)(2,1)S(1)} %fusion.9), channel_id=1, replica_groups=mesh['sub'=8,'front'=64] {'front'}, dimensions={0}, use_global_device_ids=true | all-gather | bytes 732160 | tf_op jit(solution)/shard_map/all_gather | solution.py:13
  377.2 0.1 reshape.69
  377.3 0.7 fusion.4
  378.0 67.1 %fusion.2 = bf16[48,128]{1,0:T(8,128)(2,1)S(1)} fusion(bf16[352,128]{1,0:T(8,128)(2,1)S(1)} %fusion.4), kind=kCustom, calls=%all-reduce-scatter.2 | all-reduce-scatter fusion | flops 49153 | bytes 104448
  445.2 1.9 collective-permute-start.9
  447.7 0.8 collective-permute-done.9
  448.5 0.2 concatenate.2
  448.7 12.7 %all-gather.3 = bf16[8,44,128]{2,1,0:T(8,128)(2,1)S(1)} all-gather(bf16[1,44,128]{2,1,0:T(8,128)(2,1)S(1)} %dynamic-slice_bitcast_fusion), channel_id=1, replica_groups=mesh['sub'=8,'front'=64] {'sub'}, dimensions={0}, use_global_device_ids=true | all-gather | bytes 101376 | tf_op jit(solution)/shard_map/all_gather | solution.py:17
  461.4 1.7 convolution_bitcast_fusion
  463.1 0.0 all-reduce.13.cloned.1.call-update
  463.1 0.0 all-reduce.15.cloned.1.call-start
  463.9 256.3 %all-reduce.13.cloned.1.call-done = f32[2816,128]{0,1:T(8,128)} async-done(((f32[2816,128]{0,1:T(8,128)}), f32[2816,128]{0,1:T(8,128)}) %all-reduce.13.cloned.1.call-update) | async-done | bytes 1441808
  720.1 1.0 convert_bitcast_fusion
  721.1 0.0 copy-start.2
  721.1 0.1 copy.20
  721.2 73.0 %all-gather.4 = bf16[64,44,128]{2,1,0:T(8,128)(2,1)S(1)} all-gather(bf16[1,44,128]{2,1,0:T(8,128)(2,1)S(1)} %copy.20), channel_id=1, replica_groups=mesh['sub'=8,'front'=64] {'front'}, dimensions={0}, use_global_device_ids=true | all-gather | bytes 732160 | tf_op jit(solution)/shard_map/all_gather | solution.py:13
  794.3 1.0 reshape.54
  795.3 2.5 gather_fusion
  797.8 1.3 fusion.5
  799.1 48.0 %fusion.3 = bf16[32,128]{1,0:T(8,128)(2,1)S(1)} fusion(bf16[176,128]{1,0:T(8,128)(2,1)S(1)} %fusion.5), kind=kCustom, calls=%all-reduce-scatter.3 | all-reduce-scatter fusion | flops 32769 | bytes 55296
  847.1 3.5 collective-permute-start.10
  850.6 1.4 collective-permute-start.11
  852.1 5.2 collective-permute-start.12
  857.3 0.7 collective-permute-done.12
  858.0 0.4 concatenate.3
  858.5 14.1 %all-gather.5 = bf16[8,22,128]{2,1,0:T(8,128)(2,1)S(1)} all-gather(bf16[1,22,128]{2,1,0:T(8,128)(2,1)S(1)} %fusion.12), channel_id=1, replica_groups=mesh['sub'=8,'front'=64] {'sub'}, dimensions={0}, use_global_device_ids=true | all-gather | bytes 50688 | tf_op jit(solution)/shard_map/all_gather | solution.py:17
  872.6 1.2 convolution_bitcast_fusion.1
  873.8 0.0 all-reduce.15.cloned.1.call-update
  874.5 0.7 copy.21
  875.1 250.4 %all-reduce.15.cloned.1.call-done = f32[1408,128]{0,1:T(8,128)} async-done(((f32[1408,128]{0,1:T(8,128)}), f32[1408,128]{0,1:T(8,128)}) %all-reduce.15.cloned.1.call-update) | async-done | bytes 720912
  1125.6 1.0 constant_dynamic-slice_fusion.3
  1126.5 0.7 copy.22
  (31 shorter events, 0.2 us)
Async XLA Ops:
  7.2 370.2 %copy-start = (bf16[352,2816]{1,0:T(8,128)(2,1)S(1)}, bf16[352,2816]{1,0:T(8,128)(2,1)}, u32[]{:S(2)}) copy-start(bf16[352,2816]{1,0:T(8,128)(2,1)} %param.8) | copy-start | bytes 5947396
  7.2 127.5 %copy-start.6 = (s32[1,11]{1,0:T(1,128)S(1)}, s32[1,11]{1,0:T(1,128)}, u32[]{:S(2)}) copy-start(s32[1,11]{1,0:T(1,128)} %param.11) | copy-start | bytes 136
  7.2 142.8 %copy-start.1 = (bf16[176,1408]{1,0:T(8,128)(2,1)S(1)}, bf16[176,1408]{1,0:T(8,128)(2,1)}, u32[]{:S(2)}) copy-start(bf16[176,1408]{1,0:T(8,128)(2,1)} %param.10) | copy-start | bytes 1486852
  7.2 712.9 %all-reduce.13.cloned.1.call-start = ((), (), s32[]{:S(2)}) async-start(), calls=%async_computation | async-start | bytes 2883584
  124.5 12.1 %collective-permute-start = (bf16[32,128]{1,0:T(8,128)(2,1)S(1)}, bf16[32,128]{1,0:T(8,128)(2,1)S(1)}, u32[]{:S(2)}, u32[]{:S(2)}) collective-permute-start(bf16[32,128]{1,0:T(8,128)(2,1)S(1)} %fusion), channel_id=1, source_target_pairs={{0,64},{64,128},{128,192},{192,256},{256,320},{320,384},{384,448},... | collective-permute-start | bytes 24584
  128.0 8.6 collective-permute-start.1
  129.4 7.2 collective-permute-start.2
  151.8 130.7 %copy-start.5 = (u32[512]{0:T(512)S(1)}, u32[512]{0:T(512)}, u32[]{:S(2)}) copy-start(u32[512]{0:T(512)} %constant.26) | copy-start | bytes 6148
  152.1 132.7 %copy-start.4 = (f32[44,128]{1,0:T(8,128)S(1)}, f32[44,128]{1,0:T(8,128)}, u32[]{:S(2)}) copy-start(f32[44,128]{1,0:T(8,128)} %param.6) | copy-start | bytes 67588
  274.1 7.1 collective-permute-start.8
  275.4 8.4 collective-permute-start.3
  277.3 6.5 collective-permute-start.4
  278.6 5.2 collective-permute-start.5
  279.9 3.9 collective-permute-start.6
  281.2 2.6 collective-permute-start.7
  445.2 3.3 collective-permute-start.9
  463.1 662.4 %all-reduce.15.cloned.1.call-start = ((), (), s32[]{:S(2)}) async-start(), calls=%async_computation.1 | async-start | bytes 1441792
  721.1 76.7 %copy-start.2 = (bf16[176,1408]{1,0:T(8,128)(2,1)S(1)}, bf16[176,1408]{1,0:T(8,128)(2,1)}, u32[]{:S(2)}) copy-start(bf16[176,1408]{1,0:T(8,128)(2,1)} %param.10) | copy-start | bytes 1486852
  795.3 77.3 %copy-start.3 = (bf16[176,1408]{1,0:T(8,128)(2,1)S(1)}, bf16[176,1408]{1,0:T(8,128)(2,1)}, u32[]{:S(2)}) copy-start(bf16[176,1408]{1,0:T(8,128)(2,1)} %param.9) | copy-start | bytes 1486852
  847.1 10.9 collective-permute-start.10
  850.6 7.4 collective-permute-start.11
  852.1 5.9 collective-permute-start.12
Sparse Core Ops, SparseCore 0:
  463.2 256.8 all-reduce.12
  873.9 251.5 all-reduce.14
where the time goes:
time: 1140 us; the launch traced here: 1130 us
  blocking collectives  557 us (49%)
  waiting for transfers between devices  508 us (45%)
  starting transfers between devices  30.6 us (3%)
  between operations  17.8 us (2%)
    unnamed x17, waiting for transfers between devices  508 us
    unnamed x4, blocking collectives  275 us
    all_gather x3, blocking collectives, gather_columns(): return lax.all_gather(pieces, 'front', axis=0, tiled=True)  243 us
    all_gather x3, blocking collectives, gather_rows(): return lax.all_gather(pieces, 'sub', axis=0, tiled=True)  39.7 us
    unnamed x15, starting transfers between devices  30.6 us
  transfers between devices with their start and end apart: 15, of which 4 were waited for; matrix products, arithmetic and copies ran while one was open for 0% of the time, Pallas kernels for 0%

commit v1 on v0

v1 whole, which is shorter than its diff:
```python
import jax
import jax.numpy as jnp
from jax import lax
from jax.experimental import pallas as pl
from jax.experimental.pallas import tpu as pltpu
from jax.sharding import PartitionSpec as P

RB = 128
NX, NZ, NY = 4, 16, 4
NF, NS = NX * NZ, NY * 2
CH = 176
F32, BF16 = jnp.float32, jnp.bfloat16


def rcopy(src, dst, ssem, rsem, dev):
    return pltpu.make_async_remote_copy(
        src_ref=src, dst_ref=dst, send_sem=ssem, recv_sem=rsem,
        device_id=dev, device_id_type=pl.DeviceIdType.MESH,
    )


def loop(n, fn):
    def step(i, carry):
        fn(i)
        return carry

    lax.fori_loop(0, n, step, 0)


def offset(k):
    half = (k + 1) // 2
    return NZ // 2 + half * (1 - 2 * (k % 2))


def tdot(a, b):
    return lax.dot_general(a, b, (((0,), (0,)), ((), ())), preferred_element_type=F32)


def kernel(
    rr, rl, l0_h, l1_h, ct_h, rows, rp_out, lp_out,
    l0, l1, ct, cs, cols, u, acc, own, stage, part, fl,
    ag1, ag2, ag3, ub1, ub2, ub3, xr1, xr2, xr3, zs1, zs2, zs3, zr1, zr2, zr3,
    sa1, sa2, sa3, sb1, sb2, sb3, sc1, sc2, sc3,
    ld, ag_s, ag_z, ag_x, rs_s, rs_x, rs_z, sub_s, sub_r,
):
    s, f = lax.axis_index("sub"), lax.axis_index("front")
    x, z, y, c = f // NZ, f % NZ, s // 2, s % 2

    def zdev(z2):
        return (s, x * NZ + z2)

    def xdev(e):
        return (s, ((x + e) % NX) * NZ + z)

    barrier = pltpu.get_barrier_semaphore()

    def greet(dev):
        pl.semaphore_signal(barrier, inc=1, device_id=dev, device_id_type=pl.DeviceIdType.MESH)

    loop(NZ - 1, lambda k: greet(zdev((z + offset(k)) % NZ)))
    for e in (2, 1, 3):
        greet(xdev(e))
    loop(NS - 1, lambda k: greet(((s + k + 1) % NS, f)))

    loads = [
        pltpu.make_async_copy(l1_h, l1, ld.at[0]),
        pltpu.make_async_copy(l0_h, l0, ld.at[1]),
    ]
    slots = ct.shape[0]
    for j in range(slots):
        loads.append(pltpu.make_async_copy(ct_h.at[:, j * RB:(j + 1) * RB], ct.at[j], ld.at[2 + j]))
    for load in loads:
        load.start()

    n1, n0 = rl.shape[0], rr.shape[0]
    p1, p0 = ag1.shape[1], ag2.shape[1]
    blocks = l0.shape[1] // RB

    stage[...] = jnp.zeros_like(stage)
    acc[...] = jnp.zeros_like(acc)
    part[...] = jnp.zeros_like(part)
    stage[0:n1, :] = rl[...]
    ag1[f] = stage[0:p1, :].astype(BF16)

    for load in loads:
        load.wait()
    ids = [lax.rem(rows[0, j], blocks) for j in range(slots)]
    for b in range(blocks):
        k, hit = jnp.int32(0), jnp.int32(0)
        for j in range(slots):
            same = ids[j] == b
            k = jnp.where(same, j, k)
            hit = jnp.where(same, 1, hit)
        cs[:, b * RB:(b + 1) * RB] = (ct[k].astype(F32) * hit.astype(F32)).astype(BF16)

    pl.semaphore_wait(barrier, NZ - 1 + NX - 1 + NS - 1)

    def gather(i, buf):
        def send(k):
            rcopy(buf.at[f], buf.at[f], ag_s.at[i], ag_z.at[i, z], zdev((z + offset(k)) % NZ)).start()

        loop(NZ - 1, send)

        def forward(slot):
            for e in (2, 1, 3):
                rcopy(buf.at[slot], buf.at[slot], ag_s.at[i], ag_x.at[i, e - 1], xdev(e)).start()

        forward(f)

        def relay(k):
            z2 = (z + NZ - offset(NZ - 2 - k)) % NZ
            slot = x * NZ + z2
            rcopy(buf.at[slot], buf.at[slot], ag_s.at[i], ag_z.at[i, z2], zdev(z2)).wait_recv()
            forward(slot)

        loop(NZ - 1, relay)
        for e in (1, 3, 2):
            got = buf.at[pl.ds(((x + NX - e) % NX) * NZ, NZ)]
            rcopy(got, got, ag_s.at[i], ag_x.at[i, e - 1], xdev(e)).wait_recv()

    def gather_done(i, buf):
        sent = buf.at[pl.ds(0, NF - 1)]
        rcopy(sent, sent, ag_s.at[i], ag_x.at[i, 0], xdev(1)).wait_send()

    def compact(buf, n):
        q = 88 // n

        def put(i):
            pieces = [buf[i * q + j].astype(F32)[:n] for j in range(q)]
            cols[pl.ds(pl.multiple_of(i * 88, 8), 88), :] = jnp.concatenate(pieces, axis=0)

        loop(NF // q, put)

    def scatter(i, n, pad, ub, xr, zs, zr):
        nc = ub.shape[0] // NX
        g = CH // n

        def cast(k):
            ub[k] = u[pl.ds(pl.multiple_of(k * CH, 8), CH), :].astype(BF16)

        loop(NX * nc, cast)
        far = ((z + NZ // 2) % NZ) // g
        order = [(far + d) % nc for d in ((0, 1, 3, 2) if nc == 4 else (0, 1))]
        for t in order:
            for e in (2, 1, 3):
                rcopy(
                    ub.at[((x + e) % NX) * nc + t], xr.at[e - 1, t], rs_s.at[i, 0],
                    rs_x.at[i, (e - 1) * nc + t], xdev(e),
                ).start()
        for t in order:
            for e in (1, 3, 2):
                rcopy(
                    ub.at[x * nc + t], xr.at[e - 1, t], rs_s.at[i, 0],
                    rs_x.at[i, (e - 1) * nc + t], xdev(e),
                ).wait_recv()
            total = u[pl.ds(pl.multiple_of((x * nc + t) * CH, 8), CH), :]
            for e in (1, 3, 2):
                total = total + xr[e - 1, t].astype(F32)
            acc[0:CH, :] = total
            for j in range(g):
                z2 = t * g + j
                piece = acc[j * n:j * n + pad, :]
                zs[z2] = piece.astype(BF16)

                @pl.when(z2 == z)
                def _():
                    own[0:pad, :] = piece

                @pl.when(z2 != z)
                def _():
                    rcopy(zs.at[z2], zr.at[z], rs_s.at[i, 1], rs_z.at[i, z], zdev(z2)).start()

        def add(k):
            z2 = (z + NZ - offset(NZ - 2 - k)) % NZ
            rcopy(zs.at[z2], zr.at[z2], rs_s.at[i, 1], rs_z.at[i, z2], zdev(z2)).wait_recv()
            own[0:pad, :] = own[0:pad, :] + zr[z2].astype(F32)

        loop(NZ - 1, add)

    def scatter_done(i, ub, zs):
        nc = ub.shape[0] // NX
        sent = ub.at[pl.ds(0, (NX - 1) * nc)]
        rcopy(sent, sent, rs_s.at[i, 0], rs_x.at[i, 0], xdev(1)).wait_send()
        sent = zs.at[pl.ds(0, NZ - 1)]
        rcopy(sent, sent, rs_s.at[i, 1], rs_z.at[i, 0], xdev(1)).wait_send()

    def sub_sum(i, a, b, d):
        h = a.shape[0]
        a[...] = part[pl.ds(pl.multiple_of((1 - c) * h, 8), h), :].astype(BF16)
        first = rcopy(a, b, sub_s.at[i, 0], sub_r.at[i, 0], (s + 1 - 2 * c, f))
        first.start()
        first.wait_recv()
        mine = part[pl.ds(pl.multiple_of(c * h, 8), h), :] + b[...].astype(F32)
        d[s] = mine.astype(BF16)

        def send(k):
            rcopy(d.at[s], d.at[s], sub_s.at[i, 1], sub_r.at[i, 1], ((s + k + 1) % NS, f)).start()

        loop(NS - 1, send)
        others = d.at[pl.ds(0, NS - 1)]
        rcopy(others, others, sub_s.at[i, 1], sub_r.at[i, 1], xdev(1)).wait_recv()
        halves = []
        for core in range(2):
            total = d[core].astype(F32)
            for k in range(1, NY):
                total = total + d[2 * k + core].astype(F32)
            halves.append(total)
        return halves

    def sub_done(i, a, b, d):
        rcopy(a, b, sub_s.at[i, 0], sub_r.at[i, 0], xdev(1)).wait_send()
        others = d.at[pl.ds(0, NS - 1)]
        rcopy(others, others, sub_s.at[i, 1], sub_r.at[i, 1], xdev(1)).wait_send()

    w1, w0 = l1.shape[0], l0.shape[0]
    k1, k0 = l1.shape[1], l0.shape[1]

    gather(0, ag1)
    compact(ag1, n1)
    part[0:w1, :] = jnp.dot(l1[...], cols[0:k1, :].astype(BF16), preferred_element_type=F32)
    top, bottom = sub_sum(0, sa1, sb1, sc1)
    h1 = sa1.shape[0]
    fl[0:h1, :] = top
    fl[h1:2 * h1, :] = bottom

    flb = fl[0:w1, :].astype(BF16)

    def push(b):
        at = pl.multiple_of(b * RB, RB)
        u[pl.ds(at, RB), :] = tdot(cs[:, pl.ds(at, RB)], flb)

    loop(blocks, push)
    scatter(0, n0, p0, ub1, xr1, zs1, zr1)
    stage[0:n0, :] = rr[...] - own[0:n0, :]
    ag2[f] = stage[0:p0, :].astype(BF16)

    gather(1, ag2)
    compact(ag2, n0)
    part[0:w0, :] = jnp.dot(l0[...], cols[...].astype(BF16), preferred_element_type=F32)
    top, bottom = sub_sum(1, sa2, sb2, sc2)
    h0 = sa2.shape[0]
    part[0:h0, :] = top
    part[h0:2 * h0, :] = bottom
    frb = part[0:w0, :].astype(BF16)

    def back(b):
        at = pl.multiple_of(b * RB, RB)
        u[pl.ds(at, RB), :] = tdot(l0[:, pl.ds(at, RB)], frb)

    loop(blocks, back)
    scatter(1, n0, p0, ub2, xr2, zs2, zr2)
    rp_out[...] = own[0:n0, :]
    ag3[f] = own[0:p0, :].astype(BF16)

    gather(2, ag3)
    compact(ag3, n0)
    part[w1:w0, :] = jnp.zeros((w0 - w1, part.shape[1]), F32)
    part[0:w1, :] = jnp.dot(cs[...], cols[...].astype(BF16), preferred_element_type=F32)
    top, bottom = sub_sum(2, sa3, sb3, sc3)
    fl[0:h1, :] = fl[0:h1, :] - top
    fl[h1:2 * h1, :] = fl[h1:2 * h1, :] - bottom
    corb = fl[0:w1, :].astype(BF16)

    def back_level(b):
        at = pl.multiple_of(b * RB, RB)
        u[pl.ds(at, RB), :] = tdot(l1[:, pl.ds(at, RB)], corb)

    loop(k1 // RB, back_level)
    scatter(2, n1, p1, ub3, xr3, zs3, zr3)
    lp_out[...] = own[0:n1, :]

    for i, buf in enumerate((ag1, ag2, ag3)):
        gather_done(i, buf)
    for i, (ub, zs) in enumerate(((ub1, zs1), (ub2, zs2), (ub3, zs3))):
        scatter_done(i, ub, zs)
    for i, (a, b, d) in enumerate(((sa1, sb1, sc1), (sa2, sb2, sc2), (sa3, sb3, sc3))):
        sub_done(i, a, b, d)


def body(rr, rl, l0, l1, ct, rows):
    w = rr.shape[1]
    n0, n1 = rr.shape[0], rl.shape[0]
    p0, p1 = 48, 32
    c0, c1 = CH // n0, CH // n1
    h0, h1 = l0.shape[0] // 2, 96
    vmem = pl.BlockSpec(memory_space=pltpu.VMEM)
    hbm = pl.BlockSpec(memory_space=pl.ANY)
    slots = ct.shape[1] // RB
    scratch = [
        pltpu.VMEM(l0.shape, BF16), pltpu.VMEM(l1.shape, BF16), pltpu.VMEM((slots, ct.shape[0], RB), BF16),
        pltpu.VMEM((ct.shape[0], l0.shape[1]), BF16), pltpu.VMEM((l0.shape[1], w), F32),
        pltpu.VMEM((l0.shape[1], w), F32), pltpu.VMEM((192, w), F32), pltpu.VMEM((p0, w), F32),
        pltpu.VMEM((p0, w), F32), pltpu.VMEM((l0.shape[0], w), F32), pltpu.VMEM((2 * h1, w), F32),
    ]
    pads, chunks, halves = (p0, p0, p1), (NZ // c0, NZ // c0, NZ // c1), (h1, h0, h1)
    scratch += [pltpu.VMEM((NF, p, w), BF16) for p in (p1, p0, p0)]
    scratch += [pltpu.VMEM((NX * k, CH, w), BF16) for k in chunks]
    scratch += [pltpu.VMEM((NX - 1, k, CH, w), BF16) for k in chunks]
    scratch += [pltpu.VMEM((NZ, p, w), BF16) for p in pads]
    scratch += [pltpu.VMEM((NZ, p, w), BF16) for p in pads]
    scratch += [pltpu.VMEM((h, w), BF16) for h in halves]
    scratch += [pltpu.VMEM((h, w), BF16) for h in halves]
    scratch += [pltpu.VMEM((NS, h, w), BF16) for h in halves]
    dma = pltpu.SemaphoreType.DMA
    scratch += [
        dma((2 + slots,)), dma((3,)), dma((3, NZ)), dma((3, NX - 1)), dma((3, 2)), dma((3, (NX - 1) * max(chunks))),
        dma((3, NZ)), dma((3, 2)), dma((3, 2)),
    ]
    return pl.pallas_call(
        kernel,
        out_shape=(jax.ShapeDtypeStruct((n0, w), F32), jax.ShapeDtypeStruct((n1, w), F32)),
        in_specs=[vmem, vmem, hbm, hbm, hbm, pl.BlockSpec(memory_space=pltpu.SMEM)],
        out_specs=(vmem, vmem),
        scratch_shapes=scratch,
        compiler_params=pltpu.CompilerParams(
            collective_id=0, has_side_effects=True, vmem_limit_bytes=40 << 20
        ),
    )(rr, rl, l0, l1, ct, rows)


def solution(mesh):
    return jax.shard_map(
        body,
        mesh=mesh,
        in_specs=(
            P(("sub", "front"), None),
            P(("sub", "front"), None),
            P("front", "sub"),
            P("front", "sub"),
            P("front", "sub"),
            P("front", "sub"),
        ),
        out_specs=(P(("sub", "front"), None), P(("sub", "front"), None)),
        check_vma=False,
    )
```

time: 1140 us -> 159 us (0.14)
  blocking collectives: 557 us -> 0 us
  waiting for transfers between devices: 508 us -> 0 us
  Pallas kernels: 0 us -> 151 us
  starting transfers between devices: 30.6 us -> 0 us
  between operations: 17.8 us -> 0.65 us
    unnamed x17 -> x0, waiting for transfers between devices: 508 us -> none
    all_gather x6 -> x0, blocking collectives: 283 us -> none  [the longest x3 243 us: gather_columns(): return lax.all_gather(pieces, 'front', axis=0, tiled=True)]
    unnamed x4 -> x0, blocking collectives: 275 us -> none
    pallas_call x0 -> x1, Pallas kernels: none -> 151 us  [body(): pl.pallas_call(kernel, out_shape=(jax.ShapeDtypeStruct((n0, w), F32), jax...]
    unnamed x15 -> x0, starting transfers between devices: 30.6 us -> none
  transfers between devices with their start and end apart: 15 -> 0, of which waited for: 4 -> 0; matrix products, arithmetic and copies ran while one was open for 0% -> 0% of each run, Pallas kernels for 0% -> 0%
where the time goes in v1:
time: 159 us
  Pallas kernels  151 us (95%)
  local copies, waits for them, and re-layouts  6.91 us (4%)
    pallas_call x1, Pallas kernels, body(): pl.pallas_call(kernel, out_shape=(jax.ShapeDtypeStruct((n0, w), F32), jax...  151 us
    unnamed x14, local copies, waits for them, and re-layouts  6.91 us

profile of v1, /device:TPU:1, one launch (start us, length us, event | category | flops | bytes accessed | tf_op | source)
XLA Modules:
  0.0 158.6 jit_solution(10370801364994667985)
XLA Ops:
  0.6 0.0 copy-start
  0.6 1.5 copy-done
  2.2 0.0 copy-start.1
  2.2 1.0 copy-done.1
  3.2 0.0 copy-start.2
  3.2 1.0 copy-done.2
  4.2 0.0 copy-start.3
  4.2 0.7 copy-done.3
  5.0 0.0 copy-start.4
  5.0 0.7 copy-done.4
  5.7 0.0 copy-start.5
  5.7 0.7 copy-done.5
  6.3 151.0 %shard_map.77 = (f32[44,128]{1,0:T(8,128)S(1)}, f32[22,128]{1,0:T(8,128)S(1)}) custom-call(f32[44,128]{1,0:T(8,128)S(1)} %copy-done.3, f32[22,128]{1,0:T(8,128)S(1)} %copy-done.4, bf16[352,2816]{1,0:T(8,128)(2,1)S(1)} %copy-done, bf16[176,1408]{1,0:T(8,128)(2,1)S(1)} %copy-done.1, bf16[176,1408]{1,0:T(8,128)(2,1)S(1)} %copy-done.2, s32[1,11]{1,0:T(1,128)S(1)} %copy-done.5), custom_call_target="tpu_custom_call" | custom-call | tf_op jit(solution)/shard_map/pallas_call | solution.py:309
  157.4 0.6 copy.10
  158.0 0.6 copy.11
Async XLA Ops:
  0.6 1.6 copy-start
  2.2 1.0 copy-start.1
  3.2 1.0 copy-start.2
  4.2 0.7 copy-start.3
  5.0 0.7 copy-start.4
  5.7 0.7 copy-start.5

commit v2 on v1

v2 whole, which is shorter than its diff:
```python
import jax
import jax.numpy as jnp
from jax import lax
from jax.experimental import pallas as pl
from jax.experimental.pallas import tpu as pltpu
from jax.sharding import PartitionSpec as P

RB = 128
NX, NZ, NY = 4, 16, 4
NF, NS = NX * NZ, NY * 2
CH = 176
F32, BF16 = jnp.float32, jnp.bfloat16


def rcopy(src, dst, ssem, rsem, dev):
    return pltpu.make_async_remote_copy(
        src_ref=src, dst_ref=dst, send_sem=ssem, recv_sem=rsem,
        device_id=dev, device_id_type=pl.DeviceIdType.MESH,
    )


def loop(n, fn):
    def step(i, carry):
        fn(i)
        return carry

    lax.fori_loop(0, n, step, 0)


def offset(k):
    half = (k + 1) // 2
    return NZ // 2 + half * (1 - 2 * (k % 2))


def kernel(
    rr_h, rl_h, l0_h, l1_h, ct_h, rows, rp_out, lp_out,
    rr, rl, l0, l0t, l1, l1t, ct, cs, cst, cols, u, acc, own, stage, part, fl,
    ag1, ag2, ag3, ub1, ub2, ub3, xr1, xr2, xr3, zs1, zs2, zs3, zr1, zr2, zr3,
    sa1, sa2, sa3, sb1, sb2, sb3, sc1, sc2, sc3,
    ld, ag_s, ag_z, ag_x, rs_s, rs_x, rs_z, sub_s, sub_r,
):
    s, f = lax.axis_index("sub"), lax.axis_index("front")
    x, z, y, c = f // NZ, f % NZ, s // 2, s % 2

    def zdev(z2):
        return (s, x * NZ + z2)

    def xdev(e):
        return (s, ((x + e) % NX) * NZ + z)

    pending = []
    barrier = pltpu.get_barrier_semaphore()

    def greet(dev):
        pl.semaphore_signal(barrier, inc=1, device_id=dev, device_id_type=pl.DeviceIdType.MESH)

    loop(NZ - 1, lambda k: greet(zdev((z + offset(k)) % NZ)))
    for e in (2, 1, 3):
        greet(xdev(e))
    loop(NS - 1, lambda k: greet(((s + k + 1) % NS, f)))

    loads = [
        pltpu.make_async_copy(rl_h, rl, ld.at[0]),
        pltpu.make_async_copy(l1_h, l1, ld.at[1]),
        pltpu.make_async_copy(l0_h, l0, ld.at[2]),
        pltpu.make_async_copy(rr_h, rr, ld.at[3]),
    ]
    slots = ct.shape[0]
    for j in range(slots):
        loads.append(pltpu.make_async_copy(ct_h.at[:, j * RB:(j + 1) * RB], ct.at[j], ld.at[4 + j]))
    for load in loads:
        load.start()

    n1, n0 = rl.shape[0], rr.shape[0]
    p1, p0 = ag1.shape[1], ag2.shape[1]
    blocks = l0.shape[1] // RB

    stage[...] = jnp.zeros_like(stage)
    acc[...] = jnp.zeros_like(acc)
    part[...] = jnp.zeros_like(part)
    loads[0].wait()
    stage[0:n1, :] = rl[...]
    ag1[f] = stage[0:p1, :].astype(BF16)

    pl.semaphore_wait(barrier, NZ - 1 + NX - 1 + NS - 1)

    def gather(i, buf, n, meanwhile):
        pending.append(lambda: gather_done(i, buf))
        q = 88 // n

        def forward(slot):
            for e in (2, 1, 3):
                rcopy(buf.at[slot], buf.at[slot], ag_s.at[i], ag_x.at[i, e - 1], xdev(e)).start()

        def send(k):
            rcopy(buf.at[f], buf.at[f], ag_s.at[i], ag_z.at[i, z], zdev((z + offset(NZ - 2 - k)) % NZ)).start()

        def relay(k):
            z2 = (z + NZ - offset(NZ - 2 - k)) % NZ
            slot = x * NZ + z2
            rcopy(buf.at[slot], buf.at[slot], ag_s.at[i], ag_z.at[i, z2], zdev(z2)).wait_recv()
            forward(slot)

        def compact(quarter):
            def put(j):
                at = quarter * (NZ // q) + j
                pieces = [buf[at * q + m].astype(F32)[:n] for m in range(q)]
                cols[pl.ds(pl.multiple_of(at * 88, 8), 88), :] = jnp.concatenate(pieces, axis=0)

            loop(NZ // q, put)

        forward(f)
        loop(NZ - 1, send)
        meanwhile()
        loop(NZ - 1, relay)
        compact(x)
        for e in (1, 3, 2):
            quarter = (x + NX - e) % NX
            got = buf.at[pl.ds(quarter * NZ, NZ)]
            rcopy(got, got, ag_s.at[i], ag_x.at[i, e - 1], xdev(e)).wait_recv()
            compact(quarter)

    def gather_done(i, buf):
        sent = buf.at[pl.ds(0, NF - 1)]
        rcopy(sent, sent, ag_s.at[i], ag_x.at[i, 0], xdev(1)).wait_send()

    def scatter(i, n, pad, mat, vec, ub, xr, zs, zr):
        pending.append(lambda: scatter_done(i, ub, zs))
        nc = ub.shape[0] // NX
        g = CH // n

        def product(k):
            return jnp.dot(mat[pl.ds(pl.multiple_of(k * CH, 16), CH), :], vec, preferred_element_type=F32)

        far = ((z + NZ // 2) % NZ) // g
        order = [(far + d) % nc for d in ((0, 1, 3, 2) if nc == 4 else (0, 1))]
        for t in order:
            for e in (2, 1, 3):
                k = ((x + e) % NX) * nc + t
                ub[k] = product(k).astype(BF16)
                rcopy(
                    ub.at[k], xr.at[e - 1, t], rs_s.at[i, 0], rs_x.at[i, (e - 1) * nc + t], xdev(e),
                ).start()
        for t in order:
            u[t] = product(x * nc + t)
        for t in order:
            total = u[t]
            for e in (1, 3, 2):
                rcopy(
                    ub.at[t], xr.at[e - 1, t], rs_s.at[i, 0], rs_x.at[i, (e - 1) * nc + t], xdev(e),
                ).wait_recv()
                total = total + xr[e - 1, t].astype(F32)
            acc[0:CH, :] = total
            for j in range(g):
                z2 = t * g + j
                piece = acc[j * n:j * n + pad, :]
                zs[z2] = piece.astype(BF16)

                @pl.when(z2 == z)
                def _():
                    own[0:pad, :] = piece

                @pl.when(z2 != z)
                def _():
                    rcopy(zs.at[z2], zr.at[z], rs_s.at[i, 1], rs_z.at[i, z], zdev(z2)).start()

        def add(k):
            z2 = (z + NZ - offset(NZ - 2 - k)) % NZ
            rcopy(zs.at[z2], zr.at[z2], rs_s.at[i, 1], rs_z.at[i, z2], zdev(z2)).wait_recv()
            own[0:pad, :] = own[0:pad, :] + zr[z2].astype(F32)

        loop(NZ - 1, add)

    def scatter_done(i, ub, zs):
        nc = ub.shape[0] // NX
        sent = ub.at[pl.ds(0, (NX - 1) * nc)]
        rcopy(sent, sent, rs_s.at[i, 0], rs_x.at[i, 0], xdev(1)).wait_send()
        sent = zs.at[pl.ds(0, NZ - 1)]
        rcopy(sent, sent, rs_s.at[i, 1], rs_z.at[i, 0], xdev(1)).wait_send()

    def sub_sum(i, a, b, d, meanwhile):
        pending.append(lambda: sub_done(i, a, b, d))
        h = a.shape[0]
        a[...] = part[pl.ds(pl.multiple_of((1 - c) * h, 8), h), :].astype(BF16)
        first = rcopy(a, b, sub_s.at[i, 0], sub_r.at[i, 0], (s + 1 - 2 * c, f))
        first.start()
        first.wait_recv()
        mine = part[pl.ds(pl.multiple_of(c * h, 8), h), :] + b[...].astype(F32)
        d[s] = mine.astype(BF16)

        def send(k):
            rcopy(d.at[s], d.at[s], sub_s.at[i, 1], sub_r.at[i, 1], ((s + k + 1) % NS, f)).start()

        loop(NS - 1, send)
        meanwhile()
        others = d.at[pl.ds(0, NS - 1)]
        rcopy(others, others, sub_s.at[i, 1], sub_r.at[i, 1], xdev(1)).wait_recv()
        halves = []
        for core in range(2):
            total = d[core].astype(F32)
            for k in range(1, NY):
                total = total + d[2 * k + core].astype(F32)
            halves.append(total)
        return halves

    def sub_done(i, a, b, d):
        rcopy(a, b, sub_s.at[i, 0], sub_r.at[i, 0], xdev(1)).wait_send()
        others = d.at[pl.ds(0, NS - 1)]
        rcopy(others, others, sub_s.at[i, 1], sub_r.at[i, 1], xdev(1)).wait_send()

    w1, w0 = l1.shape[0], l0.shape[0]
    k1 = l1.shape[1]

    def transpose(mat, out):
        def put(k):
            at = pl.multiple_of(k * RB, RB)
            out[pl.ds(at, RB), :] = mat[:, pl.ds(at, RB)].T

        loop(mat.shape[1] // RB, put)

    def prepare():
        for load in loads[1:]:
            load.wait()
        ids = [lax.rem(rows[0, j], blocks) for j in range(slots)]
        for b in range(blocks):
            k, hit = jnp.int32(0), jnp.int32(0)
            for j in range(slots):
                same = ids[j] == b
                k = jnp.where(same, j, k)
                hit = jnp.where(same, 1, hit)
            cs[:, b * RB:(b + 1) * RB] = (ct[k].astype(F32) * hit.astype(F32)).astype(BF16)

    def nothing():
        pass

    gather(0, ag1, n1, prepare)
    part[0:w1, :] = jnp.dot(l1[...], cols[0:k1, :].astype(BF16), preferred_element_type=F32)
    top, bottom = sub_sum(0, sa1, sb1, sc1, lambda: transpose(cs, cst))
    h1 = sa1.shape[0]
    fl[0:h1, :] = top
    fl[h1:2 * h1, :] = bottom

    scatter(0, n0, p0, cst, fl[0:w1, :].astype(BF16), ub1, xr1, zs1, zr1)
    stage[0:n0, :] = rr[...] - own[0:n0, :]
    ag2[f] = stage[0:p0, :].astype(BF16)

    gather(1, ag2, n0, lambda: transpose(l0, l0t))
    part[0:w0, :] = jnp.dot(l0[...], cols[...].astype(BF16), preferred_element_type=F32)
    top, bottom = sub_sum(1, sa2, sb2, sc2, lambda: transpose(l1, l1t))
    h0 = sa2.shape[0]
    part[0:h0, :] = top
    part[h0:2 * h0, :] = bottom

    scatter(1, n0, p0, l0t, part[0:w0, :].astype(BF16), ub2, xr2, zs2, zr2)
    rp_out[...] = own[0:n0, :]
    ag3[f] = own[0:p0, :].astype(BF16)

    gather(2, ag3, n0, nothing)
    part[w1:w0, :] = jnp.zeros((w0 - w1, part.shape[1]), F32)
    part[0:w1, :] = jnp.dot(cs[...], cols[...].astype(BF16), preferred_element_type=F32)
    top, bottom = sub_sum(2, sa3, sb3, sc3, nothing)
    fl[0:h1, :] = fl[0:h1, :] - top
    fl[h1:2 * h1, :] = fl[h1:2 * h1, :] - bottom

    scatter(2, n1, p1, l1t, fl[0:w1, :].astype(BF16), ub3, xr3, zs3, zr3)
    lp_out[...] = own[0:n1, :]

    for fin in pending:
        fin()


def body(rr, rl, l0, l1, ct, rows):
    w = rr.shape[1]
    n0, n1 = rr.shape[0], rl.shape[0]
    p0, p1 = 48, 32
    c0, c1 = CH // n0, CH // n1
    h0, h1 = l0.shape[0] // 2, 96
    vmem = pl.BlockSpec(memory_space=pltpu.VMEM)
    hbm = pl.BlockSpec(memory_space=pl.ANY)
    slots = ct.shape[1] // RB
    scratch = [
        pltpu.VMEM(rr.shape, F32), pltpu.VMEM(rl.shape, F32),
        pltpu.VMEM(l0.shape, BF16), pltpu.VMEM(l0.shape[::-1], BF16),
        pltpu.VMEM(l1.shape, BF16), pltpu.VMEM(l1.shape[::-1], BF16), pltpu.VMEM((slots, ct.shape[0], RB), BF16),
        pltpu.VMEM((ct.shape[0], l0.shape[1]), BF16), pltpu.VMEM((l0.shape[1], ct.shape[0]), BF16),
        pltpu.VMEM((l0.shape[1], w), F32), pltpu.VMEM((NZ // min(c0, c1), CH, w), F32), pltpu.VMEM((192, w), F32), pltpu.VMEM((p0, w), F32),
        pltpu.VMEM((p0, w), F32), pltpu.VMEM((l0.shape[0], w), F32), pltpu.VMEM((2 * h1, w), F32),
    ]
    pads, chunks, halves = (p0, p0, p1), (NZ // c0, NZ // c0, NZ // c1), (h1, h0, h1)
    scratch += [pltpu.VMEM((NF, p, w), BF16) for p in (p1, p0, p0)]
    scratch += [pltpu.VMEM((NX * k, CH, w), BF16) for k in chunks]
    scratch += [pltpu.VMEM((NX - 1, k, CH, w), BF16) for k in chunks]
    scratch += [pltpu.VMEM((NZ, p, w), BF16) for p in pads]
    scratch += [pltpu.VMEM((NZ, p, w), BF16) for p in pads]
    scratch += [pltpu.VMEM((h, w), BF16) for h in halves]
    scratch += [pltpu.VMEM((h, w), BF16) for h in halves]
    scratch += [pltpu.VMEM((NS, h, w), BF16) for h in halves]
    dma = pltpu.SemaphoreType.DMA
    scratch += [
        dma((4 + slots,)), dma((3,)), dma((3, NZ)), dma((3, NX - 1)), dma((3, 2)), dma((3, (NX - 1) * max(chunks))),
        dma((3, NZ)), dma((3, 2)), dma((3, 2)),
    ]
    return pl.pallas_call(
        kernel,
        out_shape=(jax.ShapeDtypeStruct((n0, w), F32), jax.ShapeDtypeStruct((n1, w), F32)),
        in_specs=[hbm, hbm, hbm, hbm, hbm, pl.BlockSpec(memory_space=pltpu.SMEM)],
        out_specs=(vmem, vmem),
        scratch_shapes=scratch,
        compiler_params=pltpu.CompilerParams(
            collective_id=0, has_side_effects=True, vmem_limit_bytes=60 << 20
        ),
    )(rr, rl, l0, l1, ct, rows)


def solution(mesh):
    return jax.shard_map(
        body,
        mesh=mesh,
        in_specs=(
            P(("sub", "front"), None),
            P(("sub", "front"), None),
            P("front", "sub"),
            P("front", "sub"),
            P("front", "sub"),
            P("front", "sub"),
        ),
        out_specs=(P(("sub", "front"), None), P(("sub", "front"), None)),
        check_vma=False,
    )
```

time: 159 us -> 139 us (0.87)
  Pallas kernels: 151 us -> 135 us
  local copies, waits for them, and re-layouts: 6.91 us -> 2.65 us
    pallas_call x1, Pallas kernels: 151 us -> 135 us  [body(): pl.pallas_call(kernel, out_shape=(jax.ShapeDtypeStruct((n0, w), F32), jax...]
    unnamed x14 -> x2, local copies, waits for them, and re-layouts: 6.91 us -> 2.65 us
where the time goes in v2:
time: 139 us; the launch traced here: 138 us
  Pallas kernels  135 us (97%)
  local copies, waits for them, and re-layouts  2.65 us (2%)
    pallas_call x1, Pallas kernels, body(): pl.pallas_call(kernel, out_shape=(jax.ShapeDtypeStruct((n0, w), F32), jax...  135 us

profile of v2, /device:TPU:1, one launch (start us, length us, event | category | flops | bytes accessed | tf_op | source)
XLA Modules:
  0.0 138.3 jit_solution(4713359873734384311)
XLA Ops:
  0.6 135.0 %shard_map.77 = (f32[44,128]{1,0:T(8,128)}, f32[22,128]{1,0:T(8,128)}) custom-call(f32[44,128]{1,0:T(8,128)} %rr_h.1, f32[22,128]{1,0:T(8,128)} %rl_h.1, bf16[352,2816]{1,0:T(8,128)(2,1)} %l0_h.1, bf16[176,1408]{1,0:T(8,128)(2,1)} %l1_h.1, bf16[176,1408]{1,0:T(8,128)(2,1)} %ct_h.1, s32[1,11]{1,0:T(1,128)} %rows.1), custom_call_target="tpu_custom_call" | custom-call | tf_op jit(solution)/shard_map/pallas_call | solution.py:303
  135.7 1.3 copy.10
  137.0 1.3 copy.11

commit v3 on v2

--- a/solution.py
+++ b/solution.py
@@ -36,7 +36,7 @@
     rr_h, rl_h, l0_h, l1_h, ct_h, rows, rp_out, lp_out,
     rr, rl, l0, l0t, l1, l1t, ct, cs, cst, cols, u, acc, own, stage, part, fl,
     ag1, ag2, ag3, ub1, ub2, ub3, xr1, xr2, xr3, zs1, zs2, zs3, zr1, zr2, zr3,
-    sa1, sa2, sa3, sb1, sb2, sb3, sc1, sc2, sc3,
+    sd1, sd2, sd3, sa1, sa2, sa3, sa4, sb1, sb2, sb3, sb4,
     ld, ag_s, ag_z, ag_x, rs_s, rs_x, rs_z, sub_s, sub_r,
 ):
     s, f = lax.axis_index("sub"), lax.axis_index("front")
@@ -57,7 +57,9 @@
     loop(NZ - 1, lambda k: greet(zdev((z + offset(k)) % NZ)))
     for e in (2, 1, 3):
         greet(xdev(e))
-    loop(NS - 1, lambda k: greet(((s + k + 1) % NS, f)))
+    for k in (2, 1, 3):
+        greet((((y + k) % NY) * 2 + c, f))
+    greet((s + 1 - 2 * c, f))
 
     loads = [
         pltpu.make_async_copy(rl_h, rl, ld.at[0]),
@@ -77,29 +79,44 @@
 
     stage[...] = jnp.zeros_like(stage)
     acc[...] = jnp.zeros_like(acc)
-    part[...] = jnp.zeros_like(part)
     loads[0].wait()
     stage[0:n1, :] = rl[...]
     ag1[f] = stage[0:p1, :].astype(BF16)
 
-    pl.semaphore_wait(barrier, NZ - 1 + NX - 1 + NS - 1)
+    def prepare():
+        for load in loads[1:]:
+            load.wait()
+        ids = [lax.rem(rows[0, j], blocks) for j in range(slots)]
+        for b in range(blocks):
+            k, hit = jnp.int32(0), jnp.int32(0)
+            for j in range(slots):
+                same = ids[j] == b
+                k = jnp.where(same, j, k)
+                hit = jnp.where(same, 1, hit)
+            cs[:, b * RB:(b + 1) * RB] = (ct[k].astype(F32) * hit.astype(F32)).astype(BF16)
+
+    prepare()
+    pl.semaphore_wait(barrier, NZ - 1 + NX - 1 + NY)
 
     def gather(i, buf, n, meanwhile):
         pending.append(lambda: gather_done(i, buf))
         q = 88 // n
 
-        def forward(slot):
+        def slot(d):
+            return x * NZ + (z + d) % NZ
+
+        def forward(d):
             for e in (2, 1, 3):
-                rcopy(buf.at[slot], buf.at[slot], ag_s.at[i], ag_x.at[i, e - 1], xdev(e)).start()
-
-        def send(k):
-            rcopy(buf.at[f], buf.at[f], ag_s.at[i], ag_z.at[i, z], zdev((z + offset(NZ - 2 - k)) % NZ)).start()
-
-        def relay(k):
-            z2 = (z + NZ - offset(NZ - 2 - k)) % NZ
-            slot = x * NZ + z2
-            rcopy(buf.at[slot], buf.at[slot], ag_s.at[i], ag_z.at[i, z2], zdev(z2)).wait_recv()
-            forward(slot)
+                rcopy(buf.at[slot(d)], buf.at[slot(d)], ag_s.at[i], ag_x.at[i, e - 1], xdev(e)).start()
+
+        def send(d, to):
+            rcopy(
+                buf.at[slot(d)], buf.at[slot(d)], ag_s.at[i], ag_z.at[i, (z + d) % NZ], zdev((z + to) % NZ)
+            ).start()
+
+        def arrive(d):
+            d = d % NZ
+            rcopy(buf.at[slot(d)], buf.at[slot(d)], ag_s.at[i], ag_z.at[i, (z + d) % NZ], zdev((z + d) % NZ)).wait_recv()
 
         def compact(quarter):
             def put(j):
@@ -109,10 +126,30 @@
 
             loop(NZ // q, put)
 
-        forward(f)
-        loop(NZ - 1, send)
+        forward(0)
+        for to in (4, 12, 3, 13, 2, 14, 1, 15):
+            send(0, to)
         meanwhile()
-        loop(NZ - 1, relay)
+        for d in (1, 15, 2, 14):
+            arrive(d)
+            forward(d)
+        for way in (NZ - 4, 4):
+            arrive(way)
+
+            @pl.when(z % 2 == (way == 4))
+            def _():
+                send(way, NZ - way)
+
+            for m in (3, 2, 1):
+                send(way, m if way == NZ - 4 else NZ - m)
+        for d in (12, 4):
+            forward(d)
+        for d in (3, 13):
+            arrive(d)
+            forward(d)
+        for d in (5, 11, 6, 10, 7, 9, 8):
+            arrive(d)
+            forward(d)
         compact(x)
         for e in (1, 3, 2):
             quarter = (x + NX - e) % NX
@@ -178,37 +215,45 @@
         sent = zs.at[pl.ds(0, NZ - 1)]
         rcopy(sent, sent, rs_s.at[i, 1], rs_z.at[i, 0], xdev(1)).wait_send()
 
-    def sub_sum(i, a, b, d, meanwhile):
-        pending.append(lambda: sub_done(i, a, b, d))
-        h = a.shape[0]
-        a[...] = part[pl.ds(pl.multiple_of((1 - c) * h, 8), h), :].astype(BF16)
-        first = rcopy(a, b, sub_s.at[i, 0], sub_r.at[i, 0], (s + 1 - 2 * c, f))
+    def swap(i, step, a, b):
+        first = rcopy(a, b, sub_s.at[i, step], sub_r.at[i, step], (s + 1 - 2 * c, f))
         first.start()
+        pending.append(first.wait_send)
         first.wait_recv()
-        mine = part[pl.ds(pl.multiple_of(c * h, 8), h), :] + b[...].astype(F32)
-        d[s] = mine.astype(BF16)
-
-        def send(k):
-            rcopy(d.at[s], d.at[s], sub_s.at[i, 1], sub_r.at[i, 1], ((s + k + 1) % NS, f)).start()
-
-        loop(NS - 1, send)
+
+    def sum_y(i, step, mine, d, meanwhile):
+        d[y] = mine.astype(BF16)
+        for k in (2, 1, 3):
+            rcopy(
+                d.at[y], d.at[y], sub_s.at[i, step], sub_r.at[i, step], (((y + k) % NY) * 2 + c, f)
+            ).start()
         meanwhile()
-        others = d.at[pl.ds(0, NS - 1)]
-        rcopy(others, others, sub_s.at[i, 1], sub_r.at[i, 1], xdev(1)).wait_recv()
-        halves = []
-        for core in range(2):
-            total = d[core].astype(F32)
-            for k in range(1, NY):
-                total = total + d[2 * k + core].astype(F32)
-            halves.append(total)
-        return halves
-
-    def sub_done(i, a, b, d):
-        rcopy(a, b, sub_s.at[i, 0], sub_r.at[i, 0], xdev(1)).wait_send()
-        others = d.at[pl.ds(0, NS - 1)]
-        rcopy(others, others, sub_s.at[i, 1], sub_r.at[i, 1], xdev(1)).wait_send()
-
-    w1, w0 = l1.shape[0], l0.shape[0]
+        others = rcopy(
+            d.at[pl.ds(0, NY - 1)], d.at[pl.ds(0, NY - 1)], sub_s.at[i, step], sub_r.at[i, step], xdev(1)
+        )
+        pending.append(others.wait_send)
+        others.wait_recv()
+        for k in range(1, NY):
+            mine = mine + d[(y + k) % NY].astype(F32)
+        return mine
+
+    def sum_level(i, d, a, b, meanwhile):
+        total = sum_y(i, 0, part[0:CH, :], d, meanwhile)
+        a[...] = total.astype(BF16)
+        swap(i, 1, a, b)
+        return total + b[...].astype(F32)
+
+    def sum_root(i, d, a, b, a2, b2, meanwhile):
+        low, high = pl.multiple_of(c * CH, 8), pl.multiple_of((1 - c) * CH, 8)
+        a[...] = part[pl.ds(high, CH), :].astype(BF16)
+        swap(i, 0, a, b)
+        total = sum_y(i, 1, part[pl.ds(low, CH), :] + b[...].astype(F32), d, meanwhile)
+        a2[...] = total.astype(BF16)
+        swap(i, 2, a2, b2)
+        part[pl.ds(low, CH), :] = total
+        part[pl.ds(high, CH), :] = b2[...].astype(F32)
+
+    w1 = l1.shape[0]
     k1 = l1.shape[1]
 
     def transpose(mat, out):
@@ -218,55 +263,39 @@
 
         loop(mat.shape[1] // RB, put)
 
-    def prepare():
-        for load in loads[1:]:
-            load.wait()
-        ids = [lax.rem(rows[0, j], blocks) for j in range(slots)]
-        for b in range(blocks):
-            k, hit = jnp.int32(0), jnp.int32(0)
-            for j in range(slots):
-                same = ids[j] == b
-                k = jnp.where(same, j, k)
-                hit = jnp.where(same, 1, hit)
-            cs[:, b * RB:(b + 1) * RB] = (ct[k].astype(F32) * hit.astype(F32)).astype(BF16)
-
     def nothing():
         pass
 
-    gather(0, ag1, n1, prepare)
+    gather(0, ag1, n1, nothing)
     part[0:w1, :] = jnp.dot(l1[...], cols[0:k1, :].astype(BF16), preferred_element_type=F32)
-    top, bottom = sub_sum(0, sa1, sb1, sc1, lambda: transpose(cs, cst))
-    h1 = sa1.shape[0]
-    fl[0:h1, :] = top
-    fl[h1:2 * h1, :] = bottom
-
-    scatter(0, n0, p0, cst, fl[0:w1, :].astype(BF16), ub1, xr1, zs1, zr1)
+    fl[...] = sum_level(0, sd1, sa1, sb1, lambda: transpose(cs, cst))
+
+    scatter(0, n0, p0, cst, fl[...].astype(BF16), ub1, xr1, zs1, zr1)
     stage[0:n0, :] = rr[...] - own[0:n0, :]
     ag2[f] = stage[0:p0, :].astype(BF16)
 
     gather(1, ag2, n0, lambda: transpose(l0, l0t))
-    part[0:w0, :] = jnp.dot(l0[...], cols[...].astype(BF16), preferred_element_type=F32)
-    top, bottom = sub_sum(1, sa2, sb2, sc2, lambda: transpose(l1, l1t))
-    h0 = sa2.shape[0]
-    part[0:h0, :] = top
-    part[h0:2 * h0, :] = bottom
-
-    scatter(1, n0, p0, l0t, part[0:w0, :].astype(BF16), ub2, xr2, zs2, zr2)
+    part[...] = jnp.dot(l0[...], cols[...].astype(BF16), preferred_element_type=F32)
+    sum_root(1, sd2, sa2, sb2, sa4, sb4, lambda: transpose(l1, l1t))
+
+    scatter(1, n0, p0, l0t, part[...].astype(BF16), ub2, xr2, zs2, zr2)
     rp_out[...] = own[0:n0, :]
     ag3[f] = own[0:p0, :].astype(BF16)
 
     gather(2, ag3, n0, nothing)
-    part[w1:w0, :] = jnp.zeros((w0 - w1, part.shape[1]), F32)
     part[0:w1, :] = jnp.dot(cs[...], cols[...].astype(BF16), preferred_element_type=F32)
-    top, bottom = sub_sum(2, sa3, sb3, sc3, nothing)
-    fl[0:h1, :] = fl[0:h1, :] - top
-    fl[h1:2 * h1, :] = fl[h1:2 * h1, :] - bottom
-
-    scatter(2, n1, p1, l1t, fl[0:w1, :].astype(BF16), ub3, xr3, zs3, zr3)
+    fl[...] = fl[...] - sum_level(2, sd3, sa3, sb3, nothing)
+
+    scatter(2, n1, p1, l1t, fl[...].astype(BF16), ub3, xr3, zs3, zr3)
     lp_out[...] = own[0:n1, :]
 
     for fin in pending:
         fin()
+
+
+def hand_over(a, b, c, d):
+    c[...] = a[...]
+    d[...] = b[...]
 
 
 def body(rr, rl, l0, l1, ct, rows):
@@ -274,7 +303,6 @@
     n0, n1 = rr.shape[0], rl.shape[0]
     p0, p1 = 48, 32
     c0, c1 = CH // n0, CH // n1
-    h0, h1 = l0.shape[0] // 2, 96
     vmem = pl.BlockSpec(memory_space=pltpu.VMEM)
     hbm = pl.BlockSpec(memory_space=pl.ANY)
     slots = ct.shape[1] // RB
@@ -284,25 +312,24 @@
         pltpu.VMEM(l1.shape, BF16), pltpu.VMEM(l1.shape[::-1], BF16), pltpu.VMEM((slots, ct.shape[0], RB), BF16),
         pltpu.VMEM((ct.shape[0], l0.shape[1]), BF16), pltpu.VMEM((l0.shape[1], ct.shape[0]), BF16),
         pltpu.VMEM((l0.shape[1], w), F32), pltpu.VMEM((NZ // min(c0, c1), CH, w), F32), pltpu.VMEM((192, w), F32), pltpu.VMEM((p0, w), F32),
-        pltpu.VMEM((p0, w), F32), pltpu.VMEM((l0.shape[0], w), F32), pltpu.VMEM((2 * h1, w), F32),
+        pltpu.VMEM((p0, w), F32), pltpu.VMEM((l0.shape[0], w), F32), pltpu.VMEM((l1.shape[0], w), F32),
     ]
-    pads, chunks, halves = (p0, p0, p1), (NZ // c0, NZ // c0, NZ // c1), (h1, h0, h1)
+    pads, chunks = (p0, p0, p1), (NZ // c0, NZ // c0, NZ // c1)
     scratch += [pltpu.VMEM((NF, p, w), BF16) for p in (p1, p0, p0)]
     scratch += [pltpu.VMEM((NX * k, CH, w), BF16) for k in chunks]
     scratch += [pltpu.VMEM((NX - 1, k, CH, w), BF16) for k in chunks]
     scratch += [pltpu.VMEM((NZ, p, w), BF16) for p in pads]
     scratch += [pltpu.VMEM((NZ, p, w), BF16) for p in pads]
-    scratch += [pltpu.VMEM((h, w), BF16) for h in halves]
-    scratch += [pltpu.VMEM((h, w), BF16) for h in halves]
-    scratch += [pltpu.VMEM((NS, h, w), BF16) for h in halves]
+    scratch += [pltpu.VMEM((NY, CH, w), BF16) for _ in range(3)]
+    scratch += [pltpu.VMEM((CH, w), BF16) for _ in range(8)]
     dma = pltpu.SemaphoreType.DMA
     scratch += [
         dma((4 + slots,)), dma((3,)), dma((3, NZ)), dma((3, NX - 1)), dma((3, 2)), dma((3, (NX - 1) * max(chunks))),
-        dma((3, NZ)), dma((3, 2)), dma((3, 2)),
+        dma((3, NZ)), dma((3, 3)), dma((3, 3)),
     ]
-    return pl.pallas_call(
+    outs = pl.pallas_call(
         kernel,
-        out_shape=(jax.ShapeDtypeStruct((n0, w), F32), jax.ShapeDtypeStruct((n1, w), F32)),
+        out_shape=(pltpu.VMEM((n0, w), F32), pltpu.VMEM((n1, w), F32)),
         in_specs=[hbm, hbm, hbm, hbm, hbm, pl.BlockSpec(memory_space=pltpu.SMEM)],
         out_specs=(vmem, vmem),
         scratch_shapes=scratch,
@@ -310,6 +337,13 @@
             collective_id=0, has_side_effects=True, vmem_limit_bytes=60 << 20
         ),
     )(rr, rl, l0, l1, ct, rows)
+    return pl.pallas_call(
+        hand_over,
+        out_shape=(jax.ShapeDtypeStruct((n0, w), F32), jax.ShapeDtypeStruct((n1, w), F32)),
+        in_specs=[pl.BlockSpec(memory_space=pltpu.VMEM)] * 2,
+        out_specs=(vmem, vmem),
+        compiler_params=pltpu.CompilerParams(vmem_limit_bytes=1 << 20),
+    )(*outs)
 
 
 def solution(mesh):

time: 139 us -> 130 us (0.935)
  Pallas kernels: 135 us -> 128 us
  local copies, waits for them, and re-layouts: 2.65 us -> 0 us
    pallas_call x1 -> x2, Pallas kernels: 135 us -> 128 us  [the longest x1 128 us: body(): pl.pallas_call(kernel, out_shape=(pltpu.VMEM((n0, w), F32), pltpu.VMEM((n...]
    unnamed x2 -> x0, local copies, waits for them, and re-layouts: 2.65 us -> none
where the time goes in v3:
time: 130 us; the launch traced here: 129 us
  Pallas kernels  128 us (98%)
    pallas_call x1, Pallas kernels, body(): pl.pallas_call(kernel, out_shape=(pltpu.VMEM((n0, w), F32), pltpu.VMEM((n...  128 us

profile of v3, /device:TPU:1, one launch (start us, length us, event | category | flops | bytes accessed | tf_op | source)
XLA Modules:
  0.0 129.1 jit_solution(8547717756935976491)
XLA Ops:
  0.6 127.8 %shard_map.77 = (f32[44,128]{1,0:T(8,128)S(1)}, f32[22,128]{1,0:T(8,128)S(1)}) custom-call(f32[44,128]{1,0:T(8,128)} %rr_h.1, f32[22,128]{1,0:T(8,128)} %rl_h.1, bf16[352,2816]{1,0:T(8,128)(2,1)} %l0_h.1, bf16[176,1408]{1,0:T(8,128)(2,1)} %l1_h.1, bf16[176,1408]{1,0:T(8,128)(2,1)} %ct_h.1, s32[1,11]{1,0:T(1,128)} %rows.1), custom_call_target="tpu_custom_call" | custom-call | tf_op jit(solution)/shard_map/pallas_call | solution.py:330
  128.5 0.6 shard_map.78

commit v4 on v3

--- a/solution.py
+++ b/solution.py
@@ -34,7 +34,7 @@
 
 def kernel(
     rr_h, rl_h, l0_h, l1_h, ct_h, rows, rp_out, lp_out,
-    rr, rl, l0, l0t, l1, l1t, ct, cs, cst, cols, u, acc, own, stage, part, fl,
+    rr, rl, l0, l0t, l1, l1t, ct, cs, cst, cols, u, wide, own, stage, part, fl,
     ag1, ag2, ag3, ub1, ub2, ub3, xr1, xr2, xr3, zs1, zs2, zs3, zr1, zr2, zr3,
     sd1, sd2, sd3, sa1, sa2, sa3, sa4, sb1, sb2, sb3, sb4,
     ld, ag_s, ag_z, ag_x, rs_s, rs_x, rs_z, sub_s, sub_r,
@@ -78,7 +78,7 @@
     blocks = l0.shape[1] // RB
 
     stage[...] = jnp.zeros_like(stage)
-    acc[...] = jnp.zeros_like(acc)
+    wide[l0.shape[1]:, :] = jnp.zeros((16, wide.shape[1]), F32)
     loads[0].wait()
     stage[0:n1, :] = rl[...]
     ag1[f] = stage[0:p1, :].astype(BF16)
@@ -95,7 +95,29 @@
                 hit = jnp.where(same, 1, hit)
             cs[:, b * RB:(b + 1) * RB] = (ct[k].astype(F32) * hit.astype(F32)).astype(BF16)
 
+    def pieces_of(mat, n, pad, out):
+        height = mat.shape[0]
+
+        def turn(b):
+            at = pl.multiple_of(b * RB, RB)
+            wide[pl.ds(at, RB), 0:height] = mat[:, pl.ds(at, RB)].T.astype(F32)
+
+        loop(mat.shape[1] // RB, turn)
+        q = 88 // n
+
+        def cut(j):
+            rows_j = wide[pl.ds(pl.multiple_of(j * 88, 8), 104), 0:height]
+            for m in range(q):
+                to = j * q + m
+                d = (to % NZ - z + NZ) % NZ
+                k = jnp.where(d < NZ // 2, NZ - 1 - 2 * d, 2 * d - NZ)
+                at = pl.multiple_of((to // NZ * NZ + k) * pad, 16)
+                out[pl.ds(at, pad), :] = rows_j[m * n:m * n + pad].astype(BF16)
+
+        loop(NF // q, cut)
+
     prepare()
+    pieces_of(l0, n0, p0, l0t)
     pl.semaphore_wait(barrier, NZ - 1 + NX - 1 + NY)
 
     def gather(i, buf, n, meanwhile):
@@ -161,59 +183,60 @@
         sent = buf.at[pl.ds(0, NF - 1)]
         rcopy(sent, sent, ag_s.at[i], ag_x.at[i, 0], xdev(1)).wait_send()
 
-    def scatter(i, n, pad, mat, vec, ub, xr, zs, zr):
+    def scatter(i, pad, mat, vec, ub, xr, zs, zr):
         pending.append(lambda: scatter_done(i, ub, zs))
-        nc = ub.shape[0] // NX
-        g = CH // n
-
-        def product(k):
-            return jnp.dot(mat[pl.ds(pl.multiple_of(k * CH, 16), CH), :], vec, preferred_element_type=F32)
-
-        far = ((z + NZ // 2) % NZ) // g
-        order = [(far + d) % nc for d in ((0, 1, 3, 2) if nc == 4 else (0, 1))]
-        for t in order:
+        g = 4
+
+        def product(quarter, j):
+            at = pl.multiple_of((quarter * NZ + j * g) * pad, 16)
+            return jnp.dot(mat[pl.ds(at, g * pad), :], vec, preferred_element_type=F32)
+
+        def xcopy(k, e):
+            slot = (e - 1) * NZ + k
+            return rcopy(ub.at[slot], xr.at[slot], rs_s.at[i, 0], rs_x.at[i, slot], xdev(e))
+
+        def push(j):
             for e in (2, 1, 3):
-                k = ((x + e) % NX) * nc + t
-                ub[k] = product(k).astype(BF16)
-                rcopy(
-                    ub.at[k], xr.at[e - 1, t], rs_s.at[i, 0], rs_x.at[i, (e - 1) * nc + t], xdev(e),
-                ).start()
-        for t in order:
-            u[t] = product(x * nc + t)
-        for t in order:
-            total = u[t]
+                pieces = product((x + e) % NX, j)
+                for m in range(g):
+                    ub[(e - 1) * NZ + j * g + m] = pieces[m * pad:(m + 1) * pad].astype(BF16)
+            for m in range(g):
+                for e in (2, 1, 3):
+                    xcopy(j * g + m, e).start()
+
+        def keep(j):
+            pieces = product(x, j)
+            for m in range(g):
+                u[j * g + m, 0:pad, :] = pieces[m * pad:(m + 1) * pad]
+
+        def add_x(k):
+            total = u[k, 0:pad, :]
             for e in (1, 3, 2):
-                rcopy(
-                    ub.at[t], xr.at[e - 1, t], rs_s.at[i, 0], rs_x.at[i, (e - 1) * nc + t], xdev(e),
-                ).wait_recv()
-                total = total + xr[e - 1, t].astype(F32)
-            acc[0:CH, :] = total
-            for j in range(g):
-                z2 = t * g + j
-                piece = acc[j * n:j * n + pad, :]
-                zs[z2] = piece.astype(BF16)
-
-                @pl.when(z2 == z)
-                def _():
-                    own[0:pad, :] = piece
-
-                @pl.when(z2 != z)
-                def _():
-                    rcopy(zs.at[z2], zr.at[z], rs_s.at[i, 1], rs_z.at[i, z], zdev(z2)).start()
-
-        def add(k):
-            z2 = (z + NZ - offset(NZ - 2 - k)) % NZ
-            rcopy(zs.at[z2], zr.at[z2], rs_s.at[i, 1], rs_z.at[i, z2], zdev(z2)).wait_recv()
-            own[0:pad, :] = own[0:pad, :] + zr[z2].astype(F32)
-
-        loop(NZ - 1, add)
+                xcopy(k, e).wait_recv()
+                total = total + xr[(e - 1) * NZ + k].astype(F32)
+            return total
+
+        def zcopy(k):
+            return rcopy(zs.at[k], zr.at[k], rs_s.at[i, 1], rs_z.at[i, k], zdev((z + offset(k)) % NZ))
+
+        def pass_on(k):
+            zs[k] = add_x(k).astype(BF16)
+            zcopy(k).start()
+
+        loop(NZ // g, push)
+        loop(NZ // g, keep)
+        loop(NZ - 1, pass_on)
+        own[0:pad, :] = add_x(NZ - 1)
+
+        def add_z(k):
+            zcopy(NZ - 2 - k).wait_recv()
+            own[0:pad, :] = own[0:pad, :] + zr[NZ - 2 - k].astype(F32)
+
+        loop(NZ - 1, add_z)
 
     def scatter_done(i, ub, zs):
-        nc = ub.shape[0] // NX
-        sent = ub.at[pl.ds(0, (NX - 1) * nc)]
-        rcopy(sent, sent, rs_s.at[i, 0], rs_x.at[i, 0], xdev(1)).wait_send()
-        sent = zs.at[pl.ds(0, NZ - 1)]
-        rcopy(sent, sent, rs_s.at[i, 1], rs_z.at[i, 0], xdev(1)).wait_send()
+        rcopy(ub, ub, rs_s.at[i, 0], rs_x.at[i, 0], xdev(1)).wait_send()
+        rcopy(zs, zs, rs_s.at[i, 1], rs_z.at[i, 0], xdev(1)).wait_send()
 
     def swap(i, step, a, b):
         first = rcopy(a, b, sub_s.at[i, step], sub_r.at[i, step], (s + 1 - 2 * c, f))
@@ -256,29 +279,22 @@
     w1 = l1.shape[0]
     k1 = l1.shape[1]
 
-    def transpose(mat, out):
-        def put(k):
-            at = pl.multiple_of(k * RB, RB)
-            out[pl.ds(at, RB), :] = mat[:, pl.ds(at, RB)].T
-
-        loop(mat.shape[1] // RB, put)
-
     def nothing():
         pass
 
     gather(0, ag1, n1, nothing)
     part[0:w1, :] = jnp.dot(l1[...], cols[0:k1, :].astype(BF16), preferred_element_type=F32)
-    fl[...] = sum_level(0, sd1, sa1, sb1, lambda: transpose(cs, cst))
-
-    scatter(0, n0, p0, cst, fl[...].astype(BF16), ub1, xr1, zs1, zr1)
+    fl[...] = sum_level(0, sd1, sa1, sb1, lambda: pieces_of(cs, n0, p0, cst))
+
+    scatter(0, p0, cst, fl[...].astype(BF16), ub1, xr1, zs1, zr1)
     stage[0:n0, :] = rr[...] - own[0:n0, :]
     ag2[f] = stage[0:p0, :].astype(BF16)
 
-    gather(1, ag2, n0, lambda: transpose(l0, l0t))
+    gather(1, ag2, n0, nothing)
     part[...] = jnp.dot(l0[...], cols[...].astype(BF16), preferred_element_type=F32)
-    sum_root(1, sd2, sa2, sb2, sa4, sb4, lambda: transpose(l1, l1t))
-
-    scatter(1, n0, p0, l0t, part[...].astype(BF16), ub2, xr2, zs2, zr2)
+    sum_root(1, sd2, sa2, sb2, sa4, sb4, lambda: pieces_of(l1, n1, p1, l1t))
+
+    scatter(1, p0, l0t, part[...].astype(BF16), ub2, xr2, zs2, zr2)
     rp_out[...] = own[0:n0, :]
     ag3[f] = own[0:p0, :].astype(BF16)
 
@@ -286,7 +302,7 @@
     part[0:w1, :] = jnp.dot(cs[...], cols[...].astype(BF16), preferred_element_type=F32)
     fl[...] = fl[...] - sum_level(2, sd3, sa3, sb3, nothing)
 
-    scatter(2, n1, p1, l1t, fl[...].astype(BF16), ub3, xr3, zs3, zr3)
+    scatter(2, p1, l1t, fl[...].astype(BF16), ub3, xr3, zs3, zr3)
     lp_out[...] = own[0:n1, :]
 
     for fin in pending:
@@ -302,29 +318,29 @@
     w = rr.shape[1]
     n0, n1 = rr.shape[0], rl.shape[0]
     p0, p1 = 48, 32
-    c0, c1 = CH // n0, CH // n1
     vmem = pl.BlockSpec(memory_space=pltpu.VMEM)
     hbm = pl.BlockSpec(memory_space=pl.ANY)
     slots = ct.shape[1] // RB
     scratch = [
         pltpu.VMEM(rr.shape, F32), pltpu.VMEM(rl.shape, F32),
-        pltpu.VMEM(l0.shape, BF16), pltpu.VMEM(l0.shape[::-1], BF16),
-        pltpu.VMEM(l1.shape, BF16), pltpu.VMEM(l1.shape[::-1], BF16), pltpu.VMEM((slots, ct.shape[0], RB), BF16),
-        pltpu.VMEM((ct.shape[0], l0.shape[1]), BF16), pltpu.VMEM((l0.shape[1], ct.shape[0]), BF16),
-        pltpu.VMEM((l0.shape[1], w), F32), pltpu.VMEM((NZ // min(c0, c1), CH, w), F32), pltpu.VMEM((192, w), F32), pltpu.VMEM((p0, w), F32),
+        pltpu.VMEM(l0.shape, BF16), pltpu.VMEM((NF * p0, l0.shape[0]), BF16),
+        pltpu.VMEM(l1.shape, BF16), pltpu.VMEM((NF * p1, l1.shape[0]), BF16), pltpu.VMEM((slots, ct.shape[0], RB), BF16),
+        pltpu.VMEM((ct.shape[0], l0.shape[1]), BF16), pltpu.VMEM((NF * p0, ct.shape[0]), BF16),
+        pltpu.VMEM((l0.shape[1], w), F32), pltpu.VMEM((NZ, p0, w), F32),
+        pltpu.VMEM((l0.shape[1] + 16, l0.shape[0]), F32), pltpu.VMEM((p0, w), F32),
         pltpu.VMEM((p0, w), F32), pltpu.VMEM((l0.shape[0], w), F32), pltpu.VMEM((l1.shape[0], w), F32),
     ]
-    pads, chunks = (p0, p0, p1), (NZ // c0, NZ // c0, NZ // c1)
+    pads = (p0, p0, p1)
     scratch += [pltpu.VMEM((NF, p, w), BF16) for p in (p1, p0, p0)]
-    scratch += [pltpu.VMEM((NX * k, CH, w), BF16) for k in chunks]
-    scratch += [pltpu.VMEM((NX - 1, k, CH, w), BF16) for k in chunks]
-    scratch += [pltpu.VMEM((NZ, p, w), BF16) for p in pads]
-    scratch += [pltpu.VMEM((NZ, p, w), BF16) for p in pads]
+    scratch += [pltpu.VMEM(((NX - 1) * NZ, p, w), BF16) for p in pads]
+    scratch += [pltpu.VMEM(((NX - 1) * NZ, p, w), BF16) for p in pads]
+    scratch += [pltpu.VMEM((NZ - 1, p, w), BF16) for p in pads]
+    scratch += [pltpu.VMEM((NZ - 1, p, w), BF16) for p in pads]
     scratch += [pltpu.VMEM((NY, CH, w), BF16) for _ in range(3)]
     scratch += [pltpu.VMEM((CH, w), BF16) for _ in range(8)]
     dma = pltpu.SemaphoreType.DMA
     scratch += [
-        dma((4 + slots,)), dma((3,)), dma((3, NZ)), dma((3, NX - 1)), dma((3, 2)), dma((3, (NX - 1) * max(chunks))),
+        dma((4 + slots,)), dma((3,)), dma((3, NZ)), dma((3, NX - 1)), dma((3, 2)), dma((3, (NX - 1) * NZ)),
         dma((3, NZ)), dma((3, 3)), dma((3, 3)),
     ]
     outs = pl.pallas_call(

time: 130 us -> 125 us (0.962)
  Pallas kernels: 128 us -> 124 us
    pallas_call x1, Pallas kernels: 128 us -> 123 us  [body(): pl.pallas_call(kernel, out_shape=(pltpu.VMEM((n0, w), F32), pltpu.VMEM((n...]
where the time goes in v4:
time: 125 us; the launch traced here: 124 us
  Pallas kernels  124 us (99%)
    pallas_call x1, Pallas kernels, body(): pl.pallas_call(kernel, out_shape=(pltpu.VMEM((n0, w), F32), pltpu.VMEM((n...  123 us

profile of v4, /device:TPU:1, one launch (start us, length us, event | category | flops | bytes accessed | tf_op | source)
XLA Modules:
  0.0 124.3 jit_solution(1766168098520262872)
XLA Ops:
  0.6 123.1 %shard_map.77 = (f32[44,128]{1,0:T(8,128)S(1)}, f32[22,128]{1,0:T(8,128)S(1)}) custom-call(f32[44,128]{1,0:T(8,128)} %rr_h.1, f32[22,128]{1,0:T(8,128)} %rl_h.1, bf16[352,2816]{1,0:T(8,128)(2,1)} %l0_h.1, bf16[176,1408]{1,0:T(8,128)(2,1)} %l1_h.1, bf16[176,1408]{1,0:T(8,128)(2,1)} %ct_h.1, s32[1,11]{1,0:T(1,128)} %rows.1), custom_call_target="tpu_custom_call" | custom-call | tf_op jit(solution)/shard_map/pallas_call | solution.py:346
  123.7 0.6 shard_map.78

commit v5 on v4

--- a/solution.py
+++ b/solution.py
@@ -129,16 +129,16 @@
 
         def forward(d):
             for e in (2, 1, 3):
-                rcopy(buf.at[slot(d)], buf.at[slot(d)], ag_s.at[i], ag_x.at[i, e - 1], xdev(e)).start()
+                rcopy(buf.at[slot(d)], buf.at[slot(d)], ag_s.at[i], ag_x.at[e - 1], xdev(e)).start()
 
         def send(d, to):
             rcopy(
-                buf.at[slot(d)], buf.at[slot(d)], ag_s.at[i], ag_z.at[i, (z + d) % NZ], zdev((z + to) % NZ)
+                buf.at[slot(d)], buf.at[slot(d)], ag_s.at[i], ag_z.at[(z + d) % NZ], zdev((z + to) % NZ)
             ).start()
 
         def arrive(d):
             d = d % NZ
-            rcopy(buf.at[slot(d)], buf.at[slot(d)], ag_s.at[i], ag_z.at[i, (z + d) % NZ], zdev((z + d) % NZ)).wait_recv()
+            rcopy(buf.at[slot(d)], buf.at[slot(d)], ag_s.at[i], ag_z.at[(z + d) % NZ], zdev((z + d) % NZ)).wait_recv()
 
         def compact(quarter):
             def put(j):
@@ -176,12 +176,12 @@
         for e in (1, 3, 2):
             quarter = (x + NX - e) % NX
             got = buf.at[pl.ds(quarter * NZ, NZ)]
-            rcopy(got, got, ag_s.at[i], ag_x.at[i, e - 1], xdev(e)).wait_recv()
+            rcopy(got, got, ag_s.at[i], ag_x.at[e - 1], xdev(e)).wait_recv()
             compact(quarter)
 
     def gather_done(i, buf):
         sent = buf.at[pl.ds(0, NF - 1)]
-        rcopy(sent, sent, ag_s.at[i], ag_x.at[i, 0], xdev(1)).wait_send()
+        rcopy(sent, sent, ag_s.at[i], ag_x.at[0], xdev(1)).wait_send()
 
     def scatter(i, pad, mat, vec, ub, xr, zs, zr):
         pending.append(lambda: scatter_done(i, ub, zs))
@@ -192,14 +192,14 @@
             return jnp.dot(mat[pl.ds(at, g * pad), :], vec, preferred_element_type=F32)
 
         def xcopy(k, e):
-            slot = (e - 1) * NZ + k
-            return rcopy(ub.at[slot], xr.at[slot], rs_s.at[i, 0], rs_x.at[i, slot], xdev(e))
+            slot = k * (NX - 1) + e - 1
+            return rcopy(ub.at[slot], xr.at[slot], rs_s.at[i, 0], rs_x.at[k], xdev(e))
 
         def push(j):
             for e in (2, 1, 3):
                 pieces = product((x + e) % NX, j)
                 for m in range(g):
-                    ub[(e - 1) * NZ + j * g + m] = pieces[m * pad:(m + 1) * pad].astype(BF16)
+                    ub[(j * g + m) * (NX - 1) + e - 1] = pieces[m * pad:(m + 1) * pad].astype(BF16)
             for m in range(g):
                 for e in (2, 1, 3):
                     xcopy(j * g + m, e).start()
@@ -211,13 +211,14 @@
 
         def add_x(k):
             total = u[k, 0:pad, :]
+            got = xr.at[pl.ds(k * (NX - 1), NX - 1)]
+            rcopy(got, got, rs_s.at[i, 0], rs_x.at[k], xdev(1)).wait_recv()
             for e in (1, 3, 2):
-                xcopy(k, e).wait_recv()
-                total = total + xr[(e - 1) * NZ + k].astype(F32)
+                total = total + xr[k * (NX - 1) + e - 1].astype(F32)
             return total
 
         def zcopy(k):
-            return rcopy(zs.at[k], zr.at[k], rs_s.at[i, 1], rs_z.at[i, k], zdev((z + offset(k)) % NZ))
+            return rcopy(zs.at[k], zr.at[k], rs_s.at[i, 1], rs_z.at[k], zdev((z + offset(k)) % NZ))
 
         def pass_on(k):
             zs[k] = add_x(k).astype(BF16)
@@ -235,8 +236,8 @@
         loop(NZ - 1, add_z)
 
     def scatter_done(i, ub, zs):
-        rcopy(ub, ub, rs_s.at[i, 0], rs_x.at[i, 0], xdev(1)).wait_send()
-        rcopy(zs, zs, rs_s.at[i, 1], rs_z.at[i, 0], xdev(1)).wait_send()
+        rcopy(ub, ub, rs_s.at[i, 0], rs_x.at[0], xdev(1)).wait_send()
+        rcopy(zs, zs, rs_s.at[i, 1], rs_z.at[0], xdev(1)).wait_send()
 
     def swap(i, step, a, b):
         first = rcopy(a, b, sub_s.at[i, step], sub_r.at[i, step], (s + 1 - 2 * c, f))
@@ -340,8 +341,8 @@
     scratch += [pltpu.VMEM((CH, w), BF16) for _ in range(8)]
     dma = pltpu.SemaphoreType.DMA
     scratch += [
-        dma((4 + slots,)), dma((3,)), dma((3, NZ)), dma((3, NX - 1)), dma((3, 2)), dma((3, (NX - 1) * NZ)),
-        dma((3, NZ)), dma((3, 3)), dma((3, 3)),
+        dma((4 + slots,)), dma((3,)), dma((NZ,)), dma((NX - 1,)), dma((3, 2)), dma((NZ,)),
+        dma((NZ,)), dma((3, 3)), dma((3, 3)),
     ]
     outs = pl.pallas_call(
         kernel,

time: 125 us -> 123 us (0.984)
  Pallas kernels: 124 us -> 122 us
    pallas_call x1, Pallas kernels: 123 us -> 121 us  [body(): pl.pallas_call(kernel, out_shape=(pltpu.VMEM((n0, w), F32), pltpu.VMEM((n...]
where the time goes in v5:
time: 123 us; the launch traced here: 122 us
  Pallas kernels  122 us (99%)
    pallas_call x1, Pallas kernels, body(): pl.pallas_call(kernel, out_shape=(pltpu.VMEM((n0, w), F32), pltpu.VMEM((n...  121 us

profile of v5, /device:TPU:1, one launch (start us, length us, event | category | flops | bytes accessed | tf_op | source)
XLA Modules:
  0.0 122.5 jit_solution(7644235753311627061)
XLA Ops:
  0.6 121.2 %shard_map.77 = (f32[44,128]{1,0:T(8,128)S(1)}, f32[22,128]{1,0:T(8,128)S(1)}) custom-call(f32[44,128]{1,0:T(8,128)} %rr_h.1, f32[22,128]{1,0:T(8,128)} %rl_h.1, bf16[352,2816]{1,0:T(8,128)(2,1)} %l0_h.1, bf16[176,1408]{1,0:T(8,128)(2,1)} %l1_h.1, bf16[176,1408]{1,0:T(8,128)(2,1)} %ct_h.1, s32[1,11]{1,0:T(1,128)} %rows.1), custom_call_target="tpu_custom_call" | custom-call | tf_op jit(solution)/shard_map/pallas_call | solution.py:347
  121.9 0.6 shard_map.78

commit v6 on v5

--- a/solution.py
+++ b/solution.py
@@ -69,7 +69,7 @@
     ]
     slots = ct.shape[0]
     for j in range(slots):
-        loads.append(pltpu.make_async_copy(ct_h.at[:, j * RB:(j + 1) * RB], ct.at[j], ld.at[4 + j]))
+        loads.append(pltpu.make_async_copy(ct_h.at[:, j * RB:(j + 1) * RB], ct.at[j], ld.at[4]))
     for load in loads:
         load.start()
 
@@ -84,8 +84,9 @@
     ag1[f] = stage[0:p1, :].astype(BF16)
 
     def prepare():
-        for load in loads[1:]:
+        for load in loads[1:4]:
             load.wait()
+        pltpu.make_async_copy(ct, ct, ld.at[4]).wait()
         ids = [lax.rem(rows[0, j], blocks) for j in range(slots)]
         for b in range(blocks):
             k, hit = jnp.int32(0), jnp.int32(0)
@@ -341,7 +342,7 @@
     scratch += [pltpu.VMEM((CH, w), BF16) for _ in range(8)]
     dma = pltpu.SemaphoreType.DMA
     scratch += [
-        dma((4 + slots,)), dma((3,)), dma((NZ,)), dma((NX - 1,)), dma((3, 2)), dma((NZ,)),
+        dma((5,)), dma((3,)), dma((NZ,)), dma((NX - 1,)), dma((3, 2)), dma((NZ,)),
         dma((NZ,)), dma((3, 3)), dma((3, 3)),
     ]
     outs = pl.pallas_call(

time: 123 us -> 123 us (level)
  no operation moved by 1% of the time
where the time goes in v6:
time: 123 us; the launch traced here: 122 us
  Pallas kernels  122 us (99%)
    pallas_call x1, Pallas kernels, body(): pl.pallas_call(kernel, out_shape=(pltpu.VMEM((n0, w), F32), pltpu.VMEM((n...  121 us

profile of v6, /device:TPU:1, one launch (start us, length us, event | category | flops | bytes accessed | tf_op | source)
XLA Modules:
  0.0 122.4 jit_solution(16273193836892046891)
XLA Ops:
  0.6 121.1 %shard_map.77 = (f32[44,128]{1,0:T(8,128)S(1)}, f32[22,128]{1,0:T(8,128)S(1)}) custom-call(f32[44,128]{1,0:T(8,128)} %rr_h.1, f32[22,128]{1,0:T(8,128)} %rl_h.1, bf16[352,2816]{1,0:T(8,128)(2,1)} %l0_h.1, bf16[176,1408]{1,0:T(8,128)(2,1)} %l1_h.1, bf16[176,1408]{1,0:T(8,128)(2,1)} %ct_h.1, s32[1,11]{1,0:T(1,128)} %rows.1), custom_call_target="tpu_custom_call" | custom-call | tf_op jit(solution)/shard_map/pallas_call | solution.py:348
  121.8 0.6 shard_map.78
